TPU v7x, 32 devices: a whole 2x2x4 slice. The times are simulated.
32 devices in a mesh: rows: 8 (over z, x), pos: 4 (over y, core).
Axes of the slice: x: 2, y: 2, z: 4, core: 2. Of those that a mesh axis runs over, the one named last changes fastest.
Arguments:
- tokens: bfloat16 [24, 640, 768], P('rows', 'pos'), may hold values from -6 to 6
- segments: int32 [24, 640], P('rows'), may hold values from 0 to 7, as said below
- w_query: bfloat16 [768, 768], replicated, may hold values from -0.21875 to 0.21875
- b_query: bfloat16 [768], replicated, may hold values from -3 to 3
- w_key: bfloat16 [768, 768], replicated, may hold values from -0.21875 to 0.21875
- w_value: bfloat16 [768, 768], replicated, may hold values from -0.21875 to 0.21875
- b_value: bfloat16 [768], replicated, may hold values from -3 to 3
- w_out: bfloat16 [768, 768], replicated, may hold values from -0.875 to 0.875
- b_out: bfloat16 [768], replicated, may hold values from -3 to 3
- gain_one: bfloat16 [768], replicated, may hold values from 0.5 to 1.5
- shift_one: bfloat16 [768], replicated, may hold values from -3 to 3
- w_up: bfloat16 [768, 3072], replicated, may hold values from -0.21875 to 0.21875
- b_up: bfloat16 [3072], replicated, may hold values from -3 to 3
- w_down: bfloat16 [3072, 768], replicated, may hold values from -0.109375 to 0.109375
- b_down: bfloat16 [768], replicated, may hold values from -3 to 3
- gain_two: bfloat16 [768], replicated, may hold values from 0.5 to 1.5
- shift_two: bfloat16 [768], replicated, may hold values from -3 to 3
- cotangent: bfloat16 [24, 640, 768], P('rows', 'pos'), may hold values from -6 to 6
Outputs:
- result: bfloat16 [24, 640, 768], P('rows', 'pos')
- grad_tokens: float32 [24, 640, 768], P('rows', 'pos')
- grad_w_query: float32 [768, 768], replicated
- grad_b_query: float32 [768], replicated
- grad_w_key: float32 [768, 768], replicated
- grad_w_value: float32 [768, 768], replicated
- grad_b_value: float32 [768], replicated
- grad_w_out: float32 [768, 768], replicated
- grad_b_out: float32 [768], replicated
- grad_gain_one: float32 [768], replicated
- grad_shift_one: float32 [768], replicated
- grad_w_up: float32 [768, 3072], replicated
- grad_b_up: float32 [3072], replicated
- grad_w_down: float32 [3072, 768], replicated
- grad_b_down: float32 [768], replicated
- grad_gain_two: float32 [768], replicated
- grad_shift_two: float32 [768], replicated
Inputs may be any that keep to these rules, and one draw needn't show every extreme that they name: `segments`: each row's segment numbers start at 0, never fall, and rise by at most one from a position to the next.
All inputs are finite; a program needn't handle non-finite values.
Results may differ from a plain program's by a relative error of at most 0.014.
Values may be sent and summed in bfloat16 or wider, within the bound.
A program may use at most 192 MiB of HBM per device.

v0:
```python
from functools import partial

import jax
import jax.numpy as jnp
from jax import lax
from jax.sharding import PartitionSpec as P

HEADS = 12
HEAD_DIM = 64


EPS = 1e-05
MASKED = -1000000000.0


def layer_norm(v, gain, shift):
    mean_row = jnp.mean(v, axis=-1, keepdims=True)
    centred = v - mean_row
    variance = jnp.mean(centred * centred, axis=-1, keepdims=True)
    return centred * lax.rsqrt(variance + EPS) * gain + shift


def tokens_dot(a, w):
    return jnp.einsum("rpd,de->rpe", a, w, preferred_element_type=jnp.float32)


def weight_grad(a, g):
    return jnp.einsum("rpd,rpe->de", a, g, preferred_element_type=jnp.float32)


def back_dot(g, w):
    return jnp.einsum("rpe,de->rpd", g, w, preferred_element_type=jnp.float32)


def token_sum(g):
    return jnp.sum(g.astype(jnp.float32), axis=(0, 1))


def split_heads(a):
    return a.reshape(a.shape[0], HEADS, HEAD_DIM)


def row_scores(query_row, key_row, same_row):
    raw_scores = jnp.einsum(
        "qhd,khd->hqk",
        split_heads(query_row),
        split_heads(key_row),
        preferred_element_type=jnp.float32,
    ) * HEAD_DIM ** (-0.5)
    return jnp.where(same_row[None], raw_scores, MASKED)


def attend_row(piece):
    query_row, key_row, value_row, same_row = piece
    scores = row_scores(query_row, key_row, same_row)
    row_top = jnp.max(scores, axis=-1, keepdims=True)
    exponent = jnp.exp(scores - row_top)
    row_total = jnp.sum(exponent, axis=-1, keepdims=True)
    log_total = row_top + jnp.log(row_total)
    prob_low = (exponent / row_total).astype(jnp.bfloat16)
    mixed = jnp.einsum(
        "hqk,khd->qhd", prob_low, split_heads(value_row), preferred_element_type=jnp.float32
    )
    mixed = mixed.reshape(query_row.shape[0], query_row.shape[1]).astype(jnp.bfloat16)
    return (mixed, log_total)


def score_grads(query_row, key_row, value_row, grad_row, same_row, log_total):
    prob_again = jnp.exp(row_scores(query_row, key_row, same_row) - log_total)
    grad_probs = jnp.einsum(
        "qhd,khd->hqk",
        split_heads(grad_row),
        split_heads(value_row),
        preferred_element_type=jnp.float32,
    )
    return (prob_again, grad_probs)


def attend_back(piece):
    query_row, key_row, value_row, grad_row, same_row, log_total = piece
    prob_again, grad_probs = score_grads(
        query_row, key_row, value_row, grad_row, same_row, log_total
    )
    row_inner = jnp.sum(grad_probs * prob_again, axis=-1, keepdims=True)
    grad_scores = (prob_again * (grad_probs - row_inner)).astype(jnp.bfloat16)
    grad_query = jnp.einsum(
        "hqk,khd->qhd", grad_scores, split_heads(key_row), preferred_element_type=jnp.float32
    ) * HEAD_DIM ** (-0.5)
    grad_query = grad_query.reshape(query_row.shape[0], query_row.shape[1]).astype(jnp.bfloat16)
    key_terms = jnp.einsum(
        "hqk,qhd->khd", grad_scores, split_heads(query_row), preferred_element_type=jnp.float32
    ) * HEAD_DIM ** (-0.5)
    value_terms = jnp.einsum(
        "hqk,qhd->khd",
        prob_again.astype(jnp.bfloat16),
        split_heads(grad_row),
        preferred_element_type=jnp.float32,
    )
    key_terms = key_terms.reshape(key_row.shape[0], key_row.shape[1])
    value_terms = value_terms.reshape(key_row.shape[0], key_row.shape[1])
    return (grad_query, key_terms, value_terms)


def on_device(
    tokens,
    segments,
    w_query,
    b_query,
    w_key,
    w_value,
    b_value,
    w_out,
    b_out,
    gain_one,
    shift_one,
    w_up,
    b_up,
    w_down,
    b_down,
    gain_two,
    shift_two,
    cotangent,
):
    rows_n, part_len, feature_width = tokens.shape
    first_pos = lax.axis_index("pos") * part_len
    seg_here = lax.dynamic_slice_in_dim(segments, first_pos, part_len, 1)
    same_doc = seg_here[:, :, None] == segments[:, None, :]
    gain_onef = gain_one.astype(jnp.float32)
    shift_onef = shift_one.astype(jnp.float32)
    gain_twof = gain_two.astype(jnp.float32)
    shift_twof = shift_two.astype(jnp.float32)
    queries = (tokens_dot(tokens, w_query) + b_query).astype(jnp.bfloat16)
    key_part = tokens_dot(tokens, w_key).astype(jnp.bfloat16)
    value_part = (tokens_dot(tokens, w_value) + b_value).astype(jnp.bfloat16)
    key_rows, value_rows = (
        lax.all_gather(key_part, "pos", axis=1, tiled=True),
        lax.all_gather(value_part, "pos", axis=1, tiled=True),
    )
    heads_mixed, log_total = lax.map(attend_row, (queries, key_rows, value_rows, same_doc))
    attended = tokens_dot(heads_mixed, w_out) + b_out
    resid_one = tokens.astype(jnp.float32) + attended
    normed, pull_one = jax.vjp(layer_norm, resid_one, gain_onef, shift_onef)
    normed_low = normed.astype(jnp.bfloat16)
    upper_in = tokens_dot(normed_low, w_up) + b_up
    active, pull_gelu = jax.vjp(partial(jax.nn.gelu, approximate=False), upper_in)
    active = active.astype(jnp.bfloat16)
    down_out = tokens_dot(active, w_down) + b_down
    resid_two = normed + down_out
    result, pull_two = jax.vjp(layer_norm, resid_two, gain_twof, shift_twof)
    grad_two, grad_gain_two, grad_shift_two = pull_two(cotangent.astype(jnp.float32))
    grad_down = grad_two.astype(jnp.bfloat16)
    grad_w_down = weight_grad(active, grad_down)
    grad_b_down = token_sum(grad_down)
    (grad_upper,) = pull_gelu(back_dot(grad_down, w_down))
    grad_upper = grad_upper.astype(jnp.bfloat16)
    grad_w_up = weight_grad(normed_low, grad_upper)
    grad_b_up = token_sum(grad_upper)
    grad_normed = grad_two + back_dot(grad_upper, w_up)
    grad_one, grad_gain_one, grad_shift_one = pull_one(grad_normed)
    grad_attend = grad_one.astype(jnp.bfloat16)
    grad_w_out = weight_grad(heads_mixed, grad_attend)
    grad_b_out = token_sum(grad_attend)
    grad_mixed = back_dot(grad_attend, w_out).astype(jnp.bfloat16)
    key_back_rows, value_back_rows = (key_rows, value_rows)
    grad_query, key_terms, value_terms = lax.map(
        attend_back, (queries, key_back_rows, value_back_rows, grad_mixed, same_doc, log_total)
    )
    grad_keys, grad_values = (
        lax.psum_scatter(
            key_terms.astype(jnp.bfloat16), "pos", scatter_dimension=1, tiled=True
        ).astype(jnp.float32),
        lax.psum_scatter(
            value_terms.astype(jnp.bfloat16), "pos", scatter_dimension=1, tiled=True
        ).astype(jnp.float32),
    )
    grad_keys = grad_keys.astype(jnp.bfloat16)
    grad_values = grad_values.astype(jnp.bfloat16)
    grad_w_query = weight_grad(tokens, grad_query)
    grad_b_query = token_sum(grad_query)
    grad_w_key = weight_grad(tokens, grad_keys)
    grad_w_value = weight_grad(tokens, grad_values)
    grad_b_value = token_sum(grad_values)
    grad_tokens = (
        grad_one
        + back_dot(grad_query, w_query)
        + back_dot(grad_keys, w_key)
        + back_dot(grad_values, w_value)
    )
    summed = lax.psum(
        (
            grad_w_query,
            grad_b_query,
            grad_w_key,
            grad_w_value,
            grad_b_value,
            grad_w_out,
            grad_b_out,
            grad_gain_one,
            grad_shift_one,
            grad_w_up,
            grad_b_up,
            grad_w_down,
            grad_b_down,
            grad_gain_two,
            grad_shift_two,
        ),
        ("rows", "pos"),
    )
    (
        grad_w_query,
        grad_b_query,
        grad_w_key,
        grad_w_value,
        grad_b_value,
        grad_w_out,
        grad_b_out,
        grad_gain_one,
        grad_shift_one,
        grad_w_up,
        grad_b_up,
        grad_w_down,
        grad_b_down,
        grad_gain_two,
        grad_shift_two,
    ) = summed
    return (
        result.astype(jnp.bfloat16),
        grad_tokens,
        grad_w_query,
        grad_b_query,
        grad_w_key,
        grad_w_value,
        grad_b_value,
        grad_w_out,
        grad_b_out,
        grad_gain_one,
        grad_shift_one,
        grad_w_up,
        grad_b_up,
        grad_w_down,
        grad_b_down,
        grad_gain_two,
        grad_shift_two,
    )


def solution(mesh):
    return jax.shard_map(
        on_device,
        mesh=mesh,
        in_specs=(
            P("rows", "pos", None),
            P("rows", None),
            P(),
            P(),
            P(),
            P(),
            P(),
            P(),
            P(),
            P(),
            P(),
            P(),
            P(),
            P(),
            P(),
            P(),
            P(),
            P("rows", "pos", None),
        ),
        out_specs=(
            P("rows", "pos", None),
            P("rows", "pos", None),
            P(),
            P(),
            P(),
            P(),
            P(),
            P(),
            P(),
            P(),
            P(),
            P(),
            P(),
            P(),
            P(),
            P(),
            P(),
        ),
        check_vma=False,
    )
```

profile of v0, /device:TPU:0, one launch (start us, length us, event | category | flops | bytes accessed | tf_op | source)
XLA Modules:
  0.0 858.6 jit_solution(15010791145762052408)
XLA Ops:
  8.1 3.1 add_convert_fusion.3
  11.3 3.0 convolution_convert_fusion.1
  14.6 1.9 add_convert_fusion.2
  19.0 22.6 %all-gather.3.cloned.1.call-done = bf16[3,640,768]{2,1,0:T(8,128)(2,1)} async-done(((bf16[3,160,768]{2,1,0:T(8,128)(2,1)}), bf16[3,640,768]{2,1,0:T(8,128)(2,1)}) %all-gather.3.cloned.1.call-update) | async-done | bytes 2949136 | tf_op jit(solution)/shard_map/all_gather | solution.py:137
  41.6 5.4 copy.73
  47.0 24.2 %all-gather.5.cloned.1.call-done = bf16[3,640,768]{2,1,0:T(8,128)(2,1)} async-done(((bf16[3,160,768]{2,1,0:T(8,128)(2,1)}), bf16[3,640,768]{2,1,0:T(8,128)(2,1)}) %all-gather.5.cloned.1.call-update) | async-done | bytes 2949136 | tf_op jit(solution)/shard_map/all_gather | solution.py:136
  71.1 5.5 copy.75
  76.7 26.4 %while.26 = (s32[]{:T(128)}, bf16[3,160,768]{1,2,0:T(8,128)(2,1)S(1)}, f32[3,12,160,1]{2,1,3,0:T(8,128)}, bf16[3,640,768]{1,2,0:T(8,128)(2,1)}, pred[3,160,640]{...) while((s32[]{:T(128)}, ...), condition=%wide.region_3.4_spmd, body=%wide.region_0.3_spmd.sunk | while | flops 329439360 | bytes 22995568 | solution.py:139
  78.7 1.7 constant_dynamic-slice_fusion.17
  81.5 1.5 fusion.120
  83.0 1.9 fusion.121
  87.5 1.7 constant_dynamic-slice_fusion.17
  90.3 1.5 fusion.120
  91.8 1.9 fusion.121
  96.3 1.7 constant_dynamic-slice_fusion.17
  99.1 1.5 fusion.120
  100.6 1.9 fusion.121
  104.5 7.6 fusion.37
  112.1 13.9 %multiply_convert_fusion.1 = (bf16[3,160,3072]{2,1,0:T(8,128)(2,1)S(1)}, f32[3,160,3072]{2,1,0:T(8,128)S(1)}) fusion(f32[3,160,3072]{2,1,0:T(8,128)S(1)} %get-tuple-element.300, f32[3072]{0:T(1024)S(1)} %convert_element_type.139, u8[160,3072]{1,0:T(8,128)(4,1)S(1)} %get-tuple-element.217, u8[160,3072]{1,0:T(8,128)(4,1)S(1)} %get-tuple-element.216), kind=kLoop, calls=%fused_computation.47 | loop fusion | flops 104693760 | bytes 15740928 | tf_op jit(solution)/shard_map/convert_element_type | solution.py:146
  126.1 2.7 fusion.65
  131.3 2.1 convert_reduce_fusion.4
  133.5 7.6 convert_reduce_fusion
  141.1 7.2 multiply_reduce_fusion.1
  149.9 1.6 convolution_convert_fusion
  152.7 74.0 %while.27 = (s32[]{:T(128)}, bf16[3,160,768]{1,2,0:T(8,128)(2,1)}, bf16[3,640,768]{2,1,0:T(8,128)(2,1)}, bf16[3,640,768]{2,1,0:T(8,128)(2,1)}, bf16[3,640,768]{1...) while((s32[]{:T(128)}, bf16[3,160,768]{1,2,0:T(8,128)(2,1)}, ...), condition=%wide.region_14.15_spmd, body=%wide.region_12.14_spmd.sunk | while | flops 806090880 | bytes 96953104 | solution.py:165
  160.3 2.6 fusion.134
  162.8 2.3 copy.133
  165.1 4.6 multiply_reduce_fusion.6
  169.8 1.4 multiply_convert_fusion.3
  171.2 1.8 fusion.133
  174.2 1.8 constant_dynamic-update-slice_fusion.8
  176.0 1.4 constant_dynamic-update-slice_fusion.9
  184.9 2.6 fusion.134
  187.4 2.3 copy.133
  189.8 4.6 multiply_reduce_fusion.6
  195.8 1.8 fusion.133
  198.9 1.8 constant_dynamic-update-slice_fusion.8
  200.6 1.5 constant_dynamic-update-slice_fusion.9
  209.5 2.6 fusion.134
  212.1 2.3 copy.133
  214.4 4.6 multiply_reduce_fusion.6
  220.4 1.8 fusion.133
  223.5 1.8 constant_dynamic-update-slice_fusion.8
  226.7 6.4 copy.86
  233.1 4.4 copy.83
  239.4 2.2 convolution_bitcast_fusion.2
  241.7 2.2 convolution_bitcast_fusion.3
  245.0 5.4 convolution_bitcast_fusion
  250.4 5.5 convolution_bitcast_fusion.1
  256.0 127.0 %all-reduce.10.cloned.1.call-done = (bf16[3,640,768]{2,0,1:T(4,128)(2,1)}, bf16[3,640,768]{2,0,1:T(4,128)(2,1)}) async-done(((bf16[3,640,768]{2,0,1:T(4,128)(2,1)}, bf16[3,640,768]{2,0,1:T(4,128)(2,1)}), (bf16[3,640,768]{2,0,1:T(4,128)(2,1)}, bf16[3,640,768]{2,0,1:T(4,128)(2,1)})) %all-reduce.10.cloned.1.call-update) | async-done | bytes 5898256
  383.0 1.5 constant_dynamic-slice_fusion.8
  384.6 2.3 convert_reduce_fusion.3
  387.8 2.2 convolution_bitcast_fusion.4
  390.0 2.2 convolution_bitcast_fusion.5
  392.6 3.6 fusion.48
  396.3 43.2 %all-reduce.2 = (f32[768]{0:T(1024)}, f32[768]{0:T(1024)}, f32[768]{0:T(1024)}, f32[768]{0:T(1024)}, f32[768]{0:T(1024)}, /*index=5*/f32[3072]{0:T(1024)}, f32[768]{0:T(1024)}, f32[768]{0:T(1024)}, f32[768]{0:T(1024)}) all-reduce(f32[768]{0:T(1024)S(1)} %convert_reduce_fusion.1, ...), channel_id=1, replica_groups=mesh['rows'=8,'pos'=4] {'rows','pos'}, use_global_device_ids=true, to_apply=%region_19.20 | all-reduce | flops 9216 | bytes 73728 | tf_op jit(solution)/shard_map/psum | solution.py:189
  439.5 2.5 fusion.45
  442.0 3.4 add_add_fusion.2
  445.4 383.4 %all-reduce.8.cloned.1.call-done = (f32[768,768]{0,1:T(8,128)}, f32[768,768]{0,1:T(8,128)}, f32[768,768]{0,1:T(8,128)}, f32[768,768]{1,0:T(8,128)}, f32[768,3072]{1,0:T(8,128)}, /*index=5*/f32[3072,768]{1,0:T(8,128)}) async-done(((f32[768,768]{0,1:T(8,128)}, f32[768,768]{0,1:T(8,128)}, f32[768,768]{0,1:T(8,128)}, f32[768,768]{1,0:T(8,128)}, f32[768,3072]{1,0:T(8,128)}, /*index=5*/f32[3072,768]{1,0:T(8,128)}), ...) | async-done | bytes 28311568 | tf_op jit(solution)/shard_map/psum | solution.py:189
  828.8 3.2 copy.92
  832.0 1.9 copy.93
  834.0 3.2 copy.94
  838.6 9.3 %copy.172 = f32[768,3072]{1,0:T(8,128)} copy(f32[768,3072]{1,0:T(8,128)} %get-tuple-element.494) | data formatting | bytes 18874368
  847.9 3.7 copy.173
  (232 shorter events, 56.5 us)
Async XLA Ops:
  7.2 96.0 %copy-start = (bf16[768,768]{1,0:T(8,128)(2,1)S(1)}, bf16[768,768]{1,0:T(8,128)(2,1)}, u32[]{:S(2)}) copy-start(bf16[768,768]{1,0:T(8,128)(2,1)} %param.29) | copy-start | bytes 3538948
  7.2 4.1 copy-start.45
  7.2 34.3 %all-gather.3.cloned.1.call-start = ((), (), s32[]{:S(2)}) async-start(), calls=%async_computation | async-start | bytes 3686400 | tf_op jit(solution)/shard_map/all_gather | solution.py:137
  11.2 3.3 copy-start.38
  11.2 3.3 copy-start.39
  11.2 3.3 copy-start.40
  11.2 3.3 copy-start.41
  11.2 3.3 copy-start.42
  11.2 3.4 copy-start.43
  11.2 3.4 copy-start.44
  11.2 3.4 copy-start.33
  11.2 3.4 copy-start.21
  11.3 59.9 %all-gather.5.cloned.1.call-start = ((), (), s32[]{:S(2)}) async-start(), calls=%async_computation.1 | async-start | bytes 3686400 | tf_op jit(solution)/shard_map/all_gather | solution.py:136
  14.4 368.7 %all-reduce.10.cloned.1.call-start = ((), (), s32[]{:S(2)}) async-start(), calls=%async_computation.3 | async-start | bytes 15728640
  14.5 111.5 %copy-start.34 = (f32[768]{0:T(1024)}, f32[768]{0:T(1024)S(1)}, u32[]{:S(2)}) copy-start(f32[768]{0:T(1024)S(1)} %convert_element_type.137) | copy-start | bytes 9220
  14.6 3.3 copy-start.27
  76.7 26.5 %copy-start.46 = (bf16[3,160,768]{2,1,0:T(8,128)(2,1)S(1)}, bf16[3,160,768]{2,1,0:T(8,128)(2,1)}, u32[]{:S(2)}) copy-start(bf16[3,160,768]{2,1,0:T(8,128)(2,1)} %param.22) | copy-start | bytes 2211844
  103.2 22.9 %slice-start.5 = ((s8[4718592]{0:T(1024)(128)(4,1)}), s8[4194304]{0:T(1024)(128)(4,1)S(1)}, s32[]{:S(2)}) async-start(s8[4718592]{0:T(1024)(128)(4,1)} %bitcast.194), calls=%async_computation.9 | async-start | bytes 8388608
  104.1 44.2 %copy-start.9 = (f32[3,160,768]{2,1,0:T(8,128)}, f32[3,160,768]{2,1,0:T(8,128)S(1)}, u32[]{:S(2)}) copy-start(f32[3,160,768]{2,1,0:T(8,128)S(1)} %get-tuple-element.299) | copy-start | bytes 4423684
  104.5 21.6 %slice-start.6 = ((s8[4718592]{0:T(1024)(128)(4,1)}), s8[524288]{0:T(1024)(128)(4,1)S(1)}, s32[]{:S(2)}) async-start(s8[4718592]{0:T(1024)(128)(4,1)} %bitcast.194), calls=%async_computation.10 | async-start | bytes 1048576
  126.0 2.7 copy-start.15
  126.1 2.7 copy-start.8
  133.5 7.6 copy-start.23
  141.1 7.2 copy-start.50
  149.0 3.7 copy-start.5
  149.9 2.7 copy-start.25
  155.6 7.2 copy-start.4
  160.3 2.6 copy-start.2
  162.8 6.9 slice-start
  165.1 4.6 slice-start.1
  173.0 3.0 copy-start.3
  180.2 7.2 copy-start.4
  187.4 6.9 slice-start
  189.8 4.6 slice-start.1
  197.7 3.0 copy-start.3
  204.9 7.2 copy-start.4
  209.5 2.6 copy-start.2
  212.1 6.9 slice-start
  214.4 4.6 slice-start.1
  222.3 3.0 copy-start.3
  226.7 6.4 copy-start.14
  237.5 591.3 %all-reduce.8.cloned.1.call-start = ((), (), s32[]{:S(2)}) async-start(), calls=%async_computation.2 | async-start | bytes 56623104 | tf_op jit(solution)/shard_map/psum | solution.py:189
  241.7 2.9 copy-start.16
  241.7 3.4 copy-start.24
  245.0 5.4 copy-start.10
  245.0 5.4 copy-start.35
  245.0 5.4 copy-start.51
  256.0 131.8 %copy-start.48 = (bf16[3,160,768]{2,1,0:T(8,128)(2,1)S(1)}, bf16[3,160,768]{2,1,0:T(8,128)(2,1)}, u32[]{:S(2)}) copy-start(bf16[3,160,768]{2,1,0:T(8,128)(2,1)} %param.22) | copy-start | bytes 2211844
  384.6 5.5 copy-start.22
  392.3 4.0 copy-start.28
  392.3 4.0 copy-start.29
  392.3 4.0 copy-start.30
  392.3 4.0 copy-start.31
  392.3 4.0 copy-start.32
  392.3 4.0 copy-start.36
  392.4 4.0 copy-start.37
  392.6 49.4 %copy-start.6 = (f32[3,160,768]{2,1,0:T(8,128)S(1)}, f32[3,160,768]{2,1,0:T(8,128)}, u32[]{:S(2)}) copy-start(f32[3,160,768]{2,1,0:T(8,128)} %copy-done.5) | copy-start | bytes 4423684
  396.3 45.8 %copy-start.13 = (bf16[3,160,768]{2,0,1:T(4,128)(2,1)S(1)}, bf16[3,160,768]{2,0,1:T(4,128)(2,1)}, u32[]{:S(2)}) copy-start(bf16[3,160,768]{2,0,1:T(4,128)(2,1)} %copy-done.12) | copy-start | bytes 2211844
  828.8 3.2 copy-start.18
  834.0 3.2 copy-start.17
  837.2 10.7 %slice-start.2 = ((s8[9437184]{0:T(1024)(128)(4,1)}), s8[4194304]{0:T(1024)(128)(4,1)S(1)}, s32[]{:S(2)}) async-start(s8[9437184]{0:T(1024)(128)(4,1)} %bitcast.192), calls=%async_computation.6 | async-start | bytes 8388608
  838.6 9.3 %slice-start.3 = ((s8[9437184]{0:T(1024)(128)(4,1)}), s8[4194304]{0:T(1024)(128)(4,1)S(1)}, s32[]{:S(2)}) async-start(s8[9437184]{0:T(1024)(128)(4,1)} %bitcast.192), calls=%async_computation.7 | async-start | bytes 8388608
  838.6 9.3 %slice-start.4 = ((s8[9437184]{0:T(1024)(128)(4,1)}), s8[1048576]{0:T(1024)(128)(4,1)S(1)}, s32[]{:S(2)}) async-start(s8[9437184]{0:T(1024)(128)(4,1)} %bitcast.192), calls=%async_computation.8 | async-start | bytes 2097152
  847.9 3.8 copy-start.1
  (9 other events, 16.3 us)
Sparse Core Ops, SparseCore 0:
  11.4 30.1 all-gather.2
  43.7 27.4 all-gather.4
  237.6 145.3 all-reduce.9
  392.4 436.3 all-reduce.7
where the time goes:
time: 870 us; the launch traced here: 859 us
  waiting for transfers between devices  557 us (64%)
  matrix products  105 us (12%)
  local copies, waits for them, and re-layouts  101 us (12%)
  blocking collectives  43.2 us (5%)
  other arithmetic  35.7 us (4%)
  between operations  15.5 us (2%)
    psum x1, waiting for transfers between devices, on_device(): lax.psum((grad_w_query, grad_b_query, grad_w_key, grad_w_value, grad_b_va...  383 us
    unnamed x5, waiting for transfers between devices  127 us
    psum x1, blocking collectives, on_device(): lax.psum((grad_w_query, grad_b_query, grad_w_key, grad_w_value, grad_b_va...  43.2 us
    unnamed x116, local copies, waits for them, and re-layouts  27.8 us
    dot_general x6, matrix products, back_dot(): return jnp.einsum('rpe,de->rpd', g, w, preferred_element_type=jnp.float32)  26 us
    all_gather x1, waiting for transfers between devices, on_device(): lax.all_gather(key_part, 'pos', axis=1, tiled=True)  24.2 us
    dynamic_slice x21, local copies, waits for them, and re-layouts, on_device(): lax.map(attend_row, (queries, key_rows, value_rows, same_doc))  22.8 us
    all_gather x1, waiting for transfers between devices, on_device(): lax.all_gather(value_part, 'pos', axis=1, tiled=True)  22.6 us
  transfers between devices with their start and end apart: 4, of which 4 were waited for; matrix products, arithmetic and copies ran while one was open for 4% of the time, Pallas kernels for 0%

commit v1 on v0

--- a/solution.py
+++ b/solution.py
@@ -3,6 +3,8 @@
 import jax
 import jax.numpy as jnp
 from jax import lax
+from jax.experimental import pallas as pl
+from jax.experimental.pallas import tpu as pltpu
 from jax.sharding import PartitionSpec as P
 
 HEADS = 12
@@ -101,7 +103,273 @@
     return (grad_query, key_terms, value_terms)
 
 
+MESH = pl.DeviceIdType.MESH
+
+
+def flip(value, bit):
+    return value + bit - 2 * bit * lax.rem(lax.div(value, bit), 2)
+
+
+def bit_of(value, bit):
+    return lax.rem(lax.div(value, bit), 2)
+
+
+def axis_bits(size):
+    assert size & (size - 1) == 0
+    return [1 << i for i in range(size.bit_length() - 1)]
+
+
+class Place:
+    def __init__(self):
+        self.row = lax.axis_index("rows")
+        self.pos = lax.axis_index("pos")
+
+    def partner(self, link):
+        axis, bit = link
+        if axis == "r":
+            return (flip(self.row, bit), self.pos)
+        return (self.row, flip(self.pos, bit))
+
+    def side(self, link):
+        axis, bit = link
+        return bit_of(self.row if axis == "r" else self.pos, bit)
+
+
+def window(ref, row0, rows, col0, cols):
+    return ref.at[pl.ds(row0, rows), pl.ds(col0, cols)]
+
+
+def plan_splits(rows, cols, links):
+    kinds = []
+    for _ in links:
+        if (rows // 2) % 16 == 0:
+            rows //= 2
+            kinds.append("rows")
+        elif (cols // 2) % 128 == 0:
+            cols //= 2
+            kinds.append("cols")
+        else:
+            kinds.append("whole")
+    return kinds
+
+
+def add_into(dst, left, right, rows):
+    step = 16 if rows % 48 else 48
+
+    @pl.loop(0, rows // step)
+    def _(i):
+        at = pl.ds(pl.multiple_of(i * step, step), step)
+        dst[at, :] = (
+            left[at, :].astype(jnp.float32) + right[at, :].astype(jnp.float32)
+        ).astype(dst.dtype)
+
+
+class Chunk:
+    def __init__(self, place, index, links, src, out, total, landing, send_sem, recv_sem, copy_sem):
+        self.place, self.index, self.links = place, index, links
+        self.src, self.out, self.total = src, out, total
+        self.send_sem, self.recv_sem, self.copy_sem = send_sem, recv_sem, copy_sem
+        rows, cols = src.shape
+        self.kinds = plan_splits(rows, cols, links)
+        self.landing = landing
+        self.row0, self.col0, self.rows, self.cols = 0, 0, rows, cols
+        self.trail, self.sent, self.recv = [], [], None
+        self.land_row = 0
+        self.step_no = 0
+
+    def steps(self):
+        return 2 * len(self.links) + 1
+
+    def halves(self, kind, side):
+        rows, cols = self.rows, self.cols
+        if kind == "rows":
+            rows //= 2
+            keep = (self.row0 + side * rows, self.col0)
+            give = (self.row0 + (1 - side) * rows, self.col0)
+        elif kind == "cols":
+            cols //= 2
+            keep = (self.row0, self.col0 + side * cols)
+            give = (self.row0, self.col0 + (1 - side) * cols)
+        else:
+            keep = give = (self.row0, self.col0)
+        return keep, give, rows, cols
+
+    def at(self, ref, place, rows, cols):
+        row0, col0 = place
+        if not isinstance(row0, int):
+            row0 = pl.multiple_of(row0, 16)
+        if not isinstance(col0, int):
+            col0 = pl.multiple_of(col0, 128)
+        return window(ref, row0, rows, col0, cols)
+
+    def send(self, link, src, dst):
+        slot = len(self.sent)
+        copy = pltpu.make_async_remote_copy(
+            src_ref=src,
+            dst_ref=dst,
+            send_sem=self.send_sem.at[self.index, slot],
+            recv_sem=self.recv_sem.at[self.index, slot],
+            device_id=self.place.partner(link),
+            device_id_type=MESH,
+        )
+        copy.start()
+        self.sent.append(copy)
+        self.recv = copy
+
+    def start_reduce(self, number):
+        link, kind = self.links[number], self.kinds[number]
+        keep, give, rows, cols = self.halves(kind, self.place.side(link))
+        base = self.src if number == 0 else self.total
+        land = window(self.landing, self.land_row, rows, 0, cols)
+        self.send(link, self.at(base, give, rows, cols), land)
+        self.pending = (kind, keep, rows, cols, base, land)
+        self.land_row += rows
+
+    def finish_reduce(self):
+        kind, keep, rows, cols, base, land = self.pending
+        self.recv.wait_recv()
+        if kind == "whole":
+            self.sent[-1].wait_send()
+        add_into(
+            self.at(self.total, keep, rows, cols), self.at(base, keep, rows, cols), land, rows
+        )
+        self.trail.append((kind, self.row0, self.col0, self.rows, self.cols))
+        (self.row0, self.col0), self.rows, self.cols = keep, rows, cols
+
+    def held(self, ref):
+        return self.at(ref, (self.row0, self.col0), self.rows, self.cols)
+
+    def start_gather(self, number):
+        if self.kinds[number] == "whole":
+            return
+        here = self.held(self.out)
+        self.send(self.links[number], here, here)
+
+    def finish_gather(self, number):
+        kind, self.row0, self.col0, self.rows, self.cols = self.trail.pop()
+        if kind != "whole":
+            self.recv.wait_recv()
+
+    def advance(self):
+        count, now = len(self.links), self.step_no
+        if now > 0 and now <= count:
+            self.finish_reduce()
+        elif now > count:
+            self.finish_gather(2 * count - now)
+        if now < count:
+            self.start_reduce(now)
+        elif now < 2 * count:
+            if now == count:
+                own = pltpu.make_async_copy(
+                    self.held(self.total), self.held(self.out), self.copy_sem.at[self.index]
+                )
+                own.start()
+                own.wait()
+            self.start_gather(2 * count - 1 - now)
+        else:
+            for index, copy in enumerate(self.sent):
+                if not (index < count and self.kinds[index] == "whole"):
+                    copy.wait_send()
+        self.step_no += 1
+
+
+def landing_rows(rows, cols, links):
+    total = 0
+    for kind in plan_splits(rows, cols, links):
+        if kind == "rows":
+            rows //= 2
+        total += rows
+    return total
+
+
+def greet(place, links):
+    barrier = pltpu.get_barrier_semaphore()
+    for link in links:
+        pl.semaphore_signal(barrier, inc=1, device_id=place.partner(link), device_id_type=MESH)
+    pl.semaphore_wait(barrier, len(links))
+
+
+def sum_kernel(orders, *refs):
+    count = len(orders)
+    (q_in, k_in, v_in, o_in, up_in, down_in, small_in) = refs[:7]
+    (q_out, k_out, v_out, o_out, up_out, down_out, small_out) = refs[7:14]
+    total, landing, small_land, send_sem, recv_sem, copy_sem, small_sem = refs[14:]
+    place = Place()
+    links = orders[0]
+    greet(place, links)
+    width = q_in.shape[0]
+    blocks = [(down_in, down_out, j * width, 0) for j in range(4)]
+    blocks += [(up_in, up_out, 0, j * width) for j in range(4)]
+    blocks += [(a, b, 0, 0) for a, b in ((o_in, o_out), (q_in, q_out), (k_in, k_out), (v_in, v_out))]
+    chunks = [
+        Chunk(
+            place,
+            index,
+            orders[index],
+            window(src, row0, width, col0, width),
+            window(out, row0, width, col0, width),
+            total.at[index],
+            landing.at[index],
+            send_sem,
+            recv_sem,
+            copy_sem,
+        )
+        for index, (src, out, row0, col0) in enumerate(blocks)
+    ]
+    small_out[...] = small_in[...]
+    for wave in range(chunks[0].steps()):
+        small = None
+        if wave < len(links):
+            small = pltpu.make_async_remote_copy(
+                src_ref=small_out,
+                dst_ref=small_land.at[wave],
+                send_sem=small_sem.at[0, wave],
+                recv_sem=small_sem.at[1, wave],
+                device_id=place.partner(links[wave]),
+                device_id_type=MESH,
+            )
+            small.start()
+        for chunk in chunks:
+            chunk.advance()
+        if small is not None:
+            small.wait()
+            small_out[...] += small_land[wave]
+
+
+def sum_gradients(mesh_shape, blocks, small):
+    row_bits = [("r", bit) for bit in axis_bits(mesh_shape["rows"])]
+    pos_bits = [("p", bit) for bit in axis_bits(mesh_shape["pos"])]
+    one = [pos_bits[0], row_bits[0], *pos_bits[1:], *row_bits[1:]]
+    two = [*pos_bits, *row_bits]
+    orders = [one if index % 2 == 0 else two for index in range(12)]
+    width = blocks[0].shape[0]
+    steps = len(one)
+    vmem = pl.BlockSpec(memory_space=pltpu.VMEM)
+    hbm = pl.BlockSpec(memory_space=pl.ANY)
+    return pl.pallas_call(
+        partial(sum_kernel, orders),
+        out_shape=[jax.ShapeDtypeStruct(b.shape, b.dtype) for b in blocks]
+        + [jax.ShapeDtypeStruct(small.shape, small.dtype)],
+        in_specs=[vmem] * 7,
+        out_specs=[hbm] * 6 + [vmem],
+        scratch_shapes=[
+            pltpu.VMEM((12, width, width), jnp.bfloat16),
+            pltpu.VMEM((12, landing_rows(width, width, one), width), jnp.bfloat16),
+            pltpu.VMEM((steps, *small.shape), jnp.float32),
+            pltpu.SemaphoreType.DMA((12, 2 * steps)),
+            pltpu.SemaphoreType.DMA((12, 2 * steps)),
+            pltpu.SemaphoreType.DMA((12,)),
+            pltpu.SemaphoreType.DMA((2, steps)),
+        ],
+        compiler_params=pltpu.CompilerParams(
+            collective_id=0, has_side_effects=True, vmem_limit_bytes=60 * 2**20
+        ),
+        name="sum_gradients",
+    )(*blocks, small)
+
+
 def on_device(
+    mesh_shape,
     tokens,
     segments,
     w_query,
@@ -186,43 +454,39 @@
         + back_dot(grad_keys, w_key)
         + back_dot(grad_values, w_value)
     )
-    summed = lax.psum(
-        (
-            grad_w_query,
+    small = jnp.concatenate(
+        [
             grad_b_query,
-            grad_w_key,
-            grad_w_value,
             grad_b_value,
-            grad_w_out,
             grad_b_out,
             grad_gain_one,
             grad_shift_one,
-            grad_w_up,
-            grad_b_up,
-            grad_w_down,
             grad_b_down,
             grad_gain_two,
             grad_shift_two,
-        ),
-        ("rows", "pos"),
+            grad_b_up,
+        ]
+    ).reshape(12, feature_width)
+    low = jnp.bfloat16
+    blocks = [
+        g.astype(low)
+        for g in (grad_w_query, grad_w_key, grad_w_value, grad_w_out, grad_w_up, grad_w_down)
+    ]
+    *blocks, small = sum_gradients(mesh_shape, blocks, jnp.pad(small, ((0, 4), (0, 0))))
+    grad_w_query, grad_w_key, grad_w_value, grad_w_out, grad_w_up, grad_w_down = (
+        b.astype(jnp.float32) for b in blocks
     )
     (
-        grad_w_query,
         grad_b_query,
-        grad_w_key,
-        grad_w_value,
         grad_b_value,
-        grad_w_out,
         grad_b_out,
         grad_gain_one,
         grad_shift_one,
-        grad_w_up,
-        grad_b_up,
-        grad_w_down,
         grad_b_down,
         grad_gain_two,
         grad_shift_two,
-    ) = summed
+    ) = (small[i] for i in range(8))
+    grad_b_up = small[8:12].reshape(-1)
     return (
         result.astype(jnp.bfloat16),
         grad_tokens,
@@ -246,7 +510,7 @@
 
 def solution(mesh):
     return jax.shard_map(
-        on_device,
+        partial(on_device, dict(mesh.shape)),
         mesh=mesh,
         in_specs=(
             P("rows", "pos", None),

time: 870 us -> 620 us (0.71)
  waiting for transfers between devices: 557 us -> 170 us
  Pallas kernels: 0 us -> 178 us
  blocking collectives: 43.2 us -> 0 us
  local copies, waits for them, and re-layouts: 101 us -> 74.5 us
  other arithmetic: 35.7 us -> 53.7 us
  matrix products: 105 us -> 117 us
    psum x1 -> x0, waiting for transfers between devices: 383 us -> none  [on_device(): lax.psum((grad_w_query, grad_b_query, grad_w_key, grad_w_value, grad_b_va...]
    pallas_call x0 -> x1, Pallas kernels: none -> 178 us  [sum_gradients(): pl.pallas_call(partial(sum_kernel, orders), out_shape=[jax.ShapeDtypeStru...]
    psum x1 -> x0, blocking collectives: 43.2 us -> none  [on_device(): lax.psum((grad_w_query, grad_b_query, grad_w_key, grad_w_value, grad_b_va...]
    unnamed x116 -> x108, local copies, waits for them, and re-layouts: 27.8 us -> 3.1 us
    convert_element_type x0 -> x6, other arithmetic: none -> 18.2 us  [on_device(): b.astype(jnp.float32)]
    unnamed x5 -> x4, waiting for transfers between devices: 127 us -> 122 us
  transfers between devices with their start and end apart: 4 -> 3, of which waited for: 4 -> 3; matrix products, arithmetic and copies ran while one was open for 4% -> 5% of each run, Pallas kernels for 0% -> 0%
where the time goes in v1:
time: 620 us; the launch traced here: 610 us
  Pallas kernels  178 us (29%)
  waiting for transfers between devices  170 us (27%)
  matrix products  117 us (19%)
  local copies, waits for them, and re-layouts  74.5 us (12%)
  other arithmetic  53.7 us (9%)
  between operations  15.6 us (3%)
    pallas_call x1, Pallas kernels, sum_gradients(): pl.pallas_call(partial(sum_kernel, orders), out_shape=[jax.ShapeDtypeStru...  178 us
    unnamed x4, waiting for transfers between devices  122 us
    dot_general x6, matrix products, back_dot(): return jnp.einsum('rpe,de->rpd', g, w, preferred_element_type=jnp.float32)  27.4 us
    all_gather x1, waiting for transfers between devices, on_device(): lax.all_gather(key_part, 'pos', axis=1, tiled=True)  24.2 us
    all_gather x1, waiting for transfers between devices, on_device(): lax.all_gather(value_part, 'pos', axis=1, tiled=True)  24.2 us
    dot_general x6, matrix products, tokens_dot(): return jnp.einsum('rpd,de->rpe', a, w, preferred_element_type=jnp.float32)  19.9 us
    dot_general x6, matrix products, weight_grad(): return jnp.einsum('rpd,rpe->de', a, g, preferred_element_type=jnp.float32)  19.9 us
    convert_element_type x6, other arithmetic, on_device(): b.astype(jnp.float32)  18.2 us
  transfers between devices with their start and end apart: 3, of which 3 were waited for; matrix products, arithmetic and copies ran while one was open for 5% of the time, Pallas kernels for 0%

profile of v1, /device:TPU:0, one launch (start us, length us, event | category | flops | bytes accessed | tf_op | source)
XLA Modules:
  0.0 610.2 jit_solution(15701627349477129788)
XLA Ops:
  8.1 3.1 add_convert_fusion.3
  11.3 2.8 convolution_convert_fusion.1
  14.3 1.9 add_convert_fusion.2
  17.3 24.2 %all-gather.3.cloned.1.call-done = bf16[3,640,768]{2,1,0:T(8,128)(2,1)} async-done(((bf16[3,160,768]{2,1,0:T(8,128)(2,1)}), bf16[3,640,768]{2,1,0:T(8,128)(2,1)}) %all-gather.3.cloned.1.call-update) | async-done | bytes 2949136 | tf_op jit(solution)/shard_map/all_gather | solution.py:405
  41.5 5.4 copy.73
  46.9 24.2 %all-gather.5.cloned.1.call-done = bf16[3,640,768]{2,1,0:T(8,128)(2,1)} async-done(((bf16[3,160,768]{2,1,0:T(8,128)(2,1)}), bf16[3,640,768]{2,1,0:T(8,128)(2,1)}) %all-gather.5.cloned.1.call-update) | async-done | bytes 2949136 | tf_op jit(solution)/shard_map/all_gather | solution.py:404
  71.1 5.5 copy.75
  77.7 22.8 %while.26 = (s32[]{:T(128)}, bf16[3,160,768]{1,2,0:T(8,128)(2,1)}, f32[3,12,160,1]{2,1,3,0:T(8,128)}, bf16[3,640,768]{1,2,0:T(8,128)(2,1)}, pred[3,160,640]{2,1,...) while((s32[]{:T(128)}, bf16[3,160,768]{1,2,0:T(8,128)(2,1)}, ...), condition=%wide.region_3.4_spmd, body=%wide.region_0.3_spmd.sunk | while | flops 329439360 | bytes 22849120 | solution.py:407
  77.7 1.7 constant_dynamic-slice_fusion.17
  80.5 1.5 fusion.123
  82.6 1.8 fusion.124
  85.3 1.7 constant_dynamic-slice_fusion.17
  88.1 1.5 fusion.123
  90.3 1.8 fusion.124
  92.9 1.7 constant_dynamic-slice_fusion.17
  95.7 1.5 fusion.123
  97.9 1.8 fusion.124
  100.5 2.6 fusion.67
  103.5 6.8 %fusion.37 = (u8[160,3072]{1,0:T(8,128)(4,1)S(1)}, u8[160,3072]{1,0:T(8,128)(4,1)S(1)}, f32[3,160,3072]{2,1,0:T(8,128)S(1)}) fusion(f32[3072]{0:T(1024)S(1)} %convert_element_type.183, bf16[768,3072]{1,0:T(8,128)(2,1)} %param.33, f32[3,160,768]{2,1,0:T(8,128)S(1)} %get-tuple-element.255, f32[768]{0:T(1024)S(1)} %convert_element_type.181, ...), kind=kOutput, calls=%fused_computation.99 | convolution fusion | flops 2286428160 | bytes 13096704 | tf_op jit(solution)/shard_map/rpd,de->rpe/dot_general | solution.py:26
  110.3 14.0 %multiply_convert_fusion.1 = (bf16[3,160,3072]{2,1,0:T(8,128)(2,1)S(1)}, f32[3,160,3072]{2,1,0:T(8,128)S(1)}) fusion(f32[3,160,3072]{2,1,0:T(8,128)S(1)} %get-tuple-element.256, f32[3072]{0:T(1024)S(1)} %convert_element_type.183, u8[160,3072]{1,0:T(8,128)(4,1)S(1)} %get-tuple-element.180, u8[160,3072]{1,0:T(8,128)(4,1)S(1)} %get-tuple-element.179), kind=kLoop, calls=%fused_computation.49 | loop fusion | flops 104693760 | bytes 15740928 | tf_op jit(solution)/shard_map/convert_element_type | solution.py:414
  124.4 2.7 fusion.68
  129.2 2.1 convert_reduce_fusion.4
  131.3 8.9 %convert_reduce_fusion = (f32[3072]{0:T(1024)}, bf16[3,160,3072]{2,1,0:T(8,128)(2,1)}) fusion(f32[3,160,3072]{2,1,0:T(8,128)S(1)} %get-tuple-element.242, bf16[3,160,768]{2,1,0:T(8,128)(2,1)S(1)} %get-tuple-element.234, bf16[3072,768]{1,0:T(8,128)(2,1)} %param.35, f32[3,160,3072]{2,1,0:T(8,128)S(1)} %get-tuple-element.256, f32[3072]{0:T(1024)S(1)} %convert_element_type.183), kind=kOutput, calls=%fused_computation.47 | convolution fusion | flops 2289988608 | bytes 20226048 | tf_op jit(solution)/shard_map/rpe,de->rpd/dot_general | solution.py:34
  140.2 7.0 %multiply_reduce_fusion.1 = (f32[768]{0:T(1024)}, f32[3,160]{1,0:T(4,128)S(1)}, f32[768]{0:T(1024)}, f32[3,160,768]{2,1,0:T(8,128)S(1)}) fusion(f32[3,160,768]{2,1,0:T(8,128)S(1)} %get-tuple-element.255, f32[3,160]{1,0:T(4,128)S(1)} %fusion.62, f32[3,160]{1,0:T(4,128)S(1)} %broadcast_multiply_fusion.1, f32[768]{0:T(1024)S(1)} %convert_element_type.180, ...), kind=kOutput, calls=%fused_computation.86 | convolution fusion | flops 2271188992 | bytes 12854400 | tf_op jit(solution)/shard_map/rpe,de->rpd/dot_general | solution.py:34
  148.8 1.6 convolution_convert_fusion
  151.6 81.6 %while.27 = (s32[]{:T(128)}, bf16[3,160,768]{1,2,0:T(8,128)(2,1)}, bf16[3,640,768]{2,1,0:T(8,128)(2,1)}, bf16[3,640,768]{2,1,0:T(8,128)(2,1)}, bf16[3,640,768]{1...) while((s32[]{:T(128)}, bf16[3,160,768]{1,2,0:T(8,128)(2,1)}, ...), condition=%wide.region_14.15_spmd, body=%wide.region_12.14_spmd.sunk | while | flops 806090880 | bytes 100247400 | solution.py:433
  151.6 1.8 constant_dynamic-slice_fusion.19
  153.4 3.1 fusion.135
  159.8 4.2 multiply_reduce_fusion.6
  168.0 4.8 fusion.137
  172.8 1.6 copy.140
  178.7 1.8 constant_dynamic-slice_fusion.19
  180.6 3.1 fusion.135
  186.9 4.2 multiply_reduce_fusion.6
  195.2 4.8 fusion.137
  200.0 1.6 copy.140
  205.9 1.8 constant_dynamic-slice_fusion.19
  207.7 3.1 fusion.135
  214.1 4.2 multiply_reduce_fusion.6
  222.3 4.8 fusion.137
  227.1 1.6 copy.140
  233.2 6.4 %copy.83 = bf16[3,640,768]{2,0,1:T(4,128)(2,1)} copy(bf16[3,640,768]{2,1,0:T(8,128)(2,1)} %get-tuple-element.119) | data formatting | bytes 5898240 | tf_op jit(solution)/shard_map/convert_element_type | solution.py:438
  239.6 4.5 copy.86
  246.0 1.5 convert_reduce_fusion.1
  247.5 3.2 bitcast_convert_fusion.2.refs_3_
  250.7 3.6 fusion.38.refs_0_
  254.4 3.7 fusion.51
  258.1 4.3 bitcast_convert_fusion.refs_5_
  262.5 5.0 bitcast_convert_fusion.1.refs_4_
  267.5 122.1 %all-reduce.6.cloned.1.call-done = (bf16[3,640,768]{2,0,1:T(4,128)(2,1)}, bf16[3,640,768]{2,0,1:T(4,128)(2,1)}) async-done(((bf16[3,640,768]{2,0,1:T(4,128)(2,1)}, bf16[3,640,768]{2,0,1:T(4,128)(2,1)}), (bf16[3,640,768]{2,0,1:T(4,128)(2,1)}, bf16[3,640,768]{2,0,1:T(4,128)(2,1)})) %all-reduce.6.cloned.1.call-update) | async-done | bytes 5898256
  389.6 1.9 convert_reduce_fusion.3
  391.7 1.8 fusion.40.refs_2_
  393.6 1.5 constant_dynamic-slice_fusion.8
  395.1 1.8 fusion.39.refs_1_
  397.6 178.0 %sum_gradients.1 = (bf16[768,768]{1,0:T(8,128)(2,1)}, bf16[768,768]{1,0:T(8,128)(2,1)}, bf16[768,768]{1,0:T(8,128)(2,1)}, bf16[768,768]{1,0:T(8,128)(2,1)}, bf16...) custom-call(bf16[768,768]{1,0:T(8,128)(2,1)} %fusion.38.refs_0_, ...), custom_call_target="tpu_custom_call" | custom-call | tf_op jit(solution)/shard_map/sum_gradients/pallas_call | solution.py:349
  575.6 1.7 slice_reduce_fusion
  578.1 1.9 fusion.48
  580.0 7.4 %convert_element_type.214 = f32[768,3072]{1,0:T(8,128)} convert(bf16[768,3072]{1,0:T(8,128)(2,1)} %get-tuple-element.126) | non-fusion elementwise | flops 2359296 | bytes 14155776 | tf_op jit(solution)/shard_map/convert_element_type | solution.py:477
  587.4 4.5 convert_element_type.215
  591.9 1.6 convert_element_type.210
  593.6 1.6 convert_element_type.211
  595.1 1.6 convert_element_type.212
  596.7 1.6 convert_element_type.213
  598.9 4.4 add_add_fusion.2
  (252 shorter events, 53.9 us)
Async XLA Ops:
  7.2 93.3 %copy-start = (bf16[768,768]{1,0:T(8,128)(2,1)S(1)}, bf16[768,768]{1,0:T(8,128)(2,1)}, u32[]{:S(2)}) copy-start(bf16[768,768]{1,0:T(8,128)(2,1)} %param.29) | copy-start | bytes 3538948
  7.2 4.1 copy-start.46
  7.2 34.3 %all-gather.3.cloned.1.call-start = ((), (), s32[]{:S(2)}) async-start(), calls=%async_computation | async-start | bytes 3686400 | tf_op jit(solution)/shard_map/all_gather | solution.py:405
  11.2 3.0 copy-start.39
  11.2 3.0 copy-start.21
  11.2 59.9 %all-gather.5.cloned.1.call-start = ((), (), s32[]{:S(2)}) async-start(), calls=%async_computation.1 | async-start | bytes 3686400 | tf_op jit(solution)/shard_map/all_gather | solution.py:404
  14.1 375.5 %all-reduce.6.cloned.1.call-start = ((), (), s32[]{:S(2)}) async-start(), calls=%async_computation.2 | async-start | bytes 15728640
  14.3 2.6 copy-start.43
  14.3 2.7 copy-start.44
  14.3 2.7 copy-start.45
  14.3 2.7 copy-start.27
  16.9 107.4 %copy-start.35 = (f32[768]{0:T(1024)}, f32[768]{0:T(1024)S(1)}, u32[]{:S(2)}) copy-start(f32[768]{0:T(1024)S(1)} %convert_element_type.181) | copy-start | bytes 9220
  100.5 23.9 %slice-start.4 = ((s8[4718592]{0:T(1024)(128)(4,1)}), s8[4194304]{0:T(1024)(128)(4,1)S(1)}, s32[]{:S(2)}) async-start(s8[4718592]{0:T(1024)(128)(4,1)} %bitcast.200), calls=%async_computation.7 | async-start | bytes 8388608
  103.1 44.1 %copy-start.9 = (f32[3,160,768]{2,1,0:T(8,128)}, f32[3,160,768]{2,1,0:T(8,128)S(1)}, u32[]{:S(2)}) copy-start(f32[3,160,768]{2,1,0:T(8,128)S(1)} %get-tuple-element.255) | copy-start | bytes 4423684
  103.4 43.8 %copy-start.29 = (f32[3,160]{1,0:T(4,128)}, f32[3,160]{1,0:T(4,128)S(1)}, u32[]{:S(2)}) copy-start(f32[3,160]{1,0:T(4,128)S(1)} %fusion.62) | copy-start | bytes 5764
  103.4 20.9 %slice-start.5 = ((s8[4718592]{0:T(1024)(128)(4,1)}), s8[524288]{0:T(1024)(128)(4,1)S(1)}, s32[]{:S(2)}) async-start(s8[4718592]{0:T(1024)(128)(4,1)} %bitcast.200), calls=%async_computation.8 | async-start | bytes 1048576
  124.3 2.7 copy-start.15
  124.4 2.7 copy-start.8
  131.3 8.9 %copy-start.23 = (bf16[3,160,768]{2,1,0:T(8,128)(2,1)}, bf16[3,160,768]{2,1,0:T(8,128)(2,1)S(1)}, u32[]{:S(2)}) copy-start(bf16[3,160,768]{2,1,0:T(8,128)(2,1)S(1)} %get-tuple-element.234) | copy-start | bytes 2211844
  147.8 3.8 copy-start.6
  148.8 2.7 copy-start.25
  151.6 5.0 copy-start.4
  151.6 5.0 copy-start.11
  159.7 4.2 slice-start
  159.7 4.2 slice-start.1
  175.9 2.8 copy-start.5
  175.9 2.8 copy-start.12
  178.7 5.0 copy-start.4
  178.7 5.0 copy-start.11
  186.9 4.2 slice-start
  186.9 4.2 slice-start.1
  203.1 2.8 copy-start.5
  203.1 2.8 copy-start.12
  205.9 5.0 copy-start.4
  205.9 5.0 copy-start.11
  214.0 4.2 slice-start
  214.0 4.2 slice-start.1
  230.2 2.8 copy-start.5
  230.2 2.8 copy-start.12
  233.2 6.4 %copy-start.14 = (bf16[3,640,768]{2,1,0:T(8,128)(2,1)S(1)}, bf16[3,640,768]{2,1,0:T(8,128)(2,1)}, u32[]{:S(2)}) copy-start(bf16[3,640,768]{2,1,0:T(8,128)(2,1)} %get-tuple-element.120) | copy-start | bytes 8847364
  244.1 3.4 copy-start.26
  247.5 3.2 copy-start.48
  250.7 3.7 copy-start.22
  254.4 3.7 copy-start.16
  254.4 3.7 copy-start.24
  258.0 4.4 copy-start.10
  258.0 4.4 copy-start.30
  258.1 4.4 copy-start.36
  258.1 4.4 copy-start.50
  262.4 129.1 %copy-start.31 = (f32[768]{0:T(1024)S(1)}, f32[768]{0:T(1024)}, u32[]{:S(2)}) copy-start(f32[768]{0:T(1024)} %get-tuple-element.235) | copy-start | bytes 9220
  262.4 129.2 %copy-start.38 = (f32[768]{0:T(1024)S(1)}, f32[768]{0:T(1024)}, u32[]{:S(2)}) copy-start(f32[768]{0:T(1024)} %get-tuple-element.181) | copy-start | bytes 9220
  262.5 129.2 %copy-start.37 = (f32[768]{0:T(1024)S(1)}, f32[768]{0:T(1024)}, u32[]{:S(2)}) copy-start(f32[768]{0:T(1024)} %get-tuple-element.187) | copy-start | bytes 9220
  262.5 129.2 %copy-start.32 = (f32[768]{0:T(1024)S(1)}, f32[768]{0:T(1024)}, u32[]{:S(2)}) copy-start(f32[768]{0:T(1024)} %get-tuple-element.233) | copy-start | bytes 9220
  262.5 129.2 %copy-start.28 = (f32[768]{0:T(1024)S(1)}, f32[768]{0:T(1024)}, u32[]{:S(2)}) copy-start(f32[768]{0:T(1024)} %get-tuple-element.183) | copy-start | bytes 9220
  262.5 129.2 %copy-start.33 = (f32[3072]{0:T(1024)S(1)}, f32[3072]{0:T(1024)}, u32[]{:S(2)}) copy-start(f32[3072]{0:T(1024)} %get-tuple-element.260) | copy-start | bytes 36868
  391.6 5.4 copy-start.13
  397.6 180.5 %copy-start.47 = (bf16[768,768]{1,0:T(8,128)(2,1)S(1)}, bf16[768,768]{1,0:T(8,128)(2,1)}, u32[]{:S(2)}) copy-start(bf16[768,768]{1,0:T(8,128)(2,1)} %param.26) | copy-start | bytes 3538948
  578.1 9.3 %slice-start.2 = ((s8[4718592]{0:T(1024)(128)(4,1)}), s8[4194304]{0:T(1024)(128)(4,1)S(1)}, s32[]{:S(2)}) async-start(s8[4718592]{0:T(1024)(128)(4,1)} %bitcast.198), calls=%async_computation.5 | async-start | bytes 8388608
  580.0 7.4 %slice-start.3 = ((s8[4718592]{0:T(1024)(128)(4,1)}), s8[524288]{0:T(1024)(128)(4,1)S(1)}, s32[]{:S(2)}) async-start(s8[4718592]{0:T(1024)(128)(4,1)} %bitcast.198), calls=%async_computation.6 | async-start | bytes 1048576
  587.4 4.5 copy-start.20
  591.9 3.2 copy-start.18
  593.5 3.2 copy-start.17
  595.1 3.8 copy-start.7
  598.3 5.0 copy-start.1
  (12 other events, 24.2 us)
Sparse Core Ops, SparseCore 0:
  11.4 30.1 all-gather.2
  43.6 27.4 all-gather.4
  244.2 145.3 all-reduce.5
